TPU v7x, 32 devices: a whole 2x2x4 slice. The times are simulated.
32 devices in a mesh: dp: 8 (over y, x, core), seq: 4 (over z).
Axes of the slice: x: 2, y: 2, z: 4, core: 2. Of those that a mesh axis runs over, the one named last changes fastest.
Arguments:
- hidden_in: bfloat16 [32, 512, 768], P('dp', 'seq'), may hold values from -6 to 6
- query_lengths: int32 [32], P('dp'), may hold values from 1 to 64, as said below
- doc_lengths: int32 [32], P('dp'), may hold values from 32 to 448, as said below
- w_query: bfloat16 [768, 768], replicated, may hold values from -0.109375 to 0.109375
- w_key: bfloat16 [768, 768], replicated, may hold values from -0.109375 to 0.109375
- w_value: bfloat16 [768, 768], replicated, may hold values from -0.21875 to 0.21875
- w_attn_out: bfloat16 [768, 768], replicated, may hold values from -0.875 to 0.875
- w_inner: bfloat16 [768, 3072], replicated, may hold values from -0.21875 to 0.21875
- w_outer: bfloat16 [3072, 768], replicated, may hold values from -0.109375 to 0.109375
- gain_attn: bfloat16 [768], replicated, may hold values from 0.5 to 1.5
- gain_ffn: bfloat16 [768], replicated, may hold values from 0.5 to 1.5
- bias_table: bfloat16 [32, 12], replicated, may hold values from -4 to 4
- cotangent: bfloat16 [32, 512, 768], P('dp', 'seq'), may hold values from -6 to 6
Outputs:
- layer_out: bfloat16 [32, 512, 768], P('dp', 'seq')
- grad_in: bfloat16 [32, 512, 768], P('dp', 'seq')
- grad_query: float32 [768, 768], P('dp')
- grad_key: float32 [768, 768], P('dp')
- grad_value: float32 [768, 768], P('dp')
- grad_attn_out: float32 [768, 768], P('dp')
- grad_inner: float32 [768, 3072], P('dp')
- grad_outer: float32 [3072, 768], P('dp')
- grad_gain_attn: float32 [768], P('dp')
- grad_gain_ffn: float32 [768], P('dp')
- grad_table: float32 [32, 12], replicated
Inputs may be any that keep to these rules, and one draw needn't show every extreme that they name: `query_lengths`: in each aligned block of 2 rows one row has exactly 64 query tokens and fills all 512 slots. `doc_lengths`: A row's query and document tokens together take at most 512 slots; its other slots are padding. The row that fills all 512 slots has exactly 448 document tokens.
All inputs are finite; a program needn't handle non-finite values.
Results may differ from a plain program's by a relative error of at most 0.018.
Values may be sent and summed in bfloat16 or wider, within the bound.
A program may use at most 256 MiB of HBM per device.

v0:
```python
from functools import partial

import jax
import jax.numpy as jnp
from jax import lax
from jax.experimental import pallas as pl
from jax.experimental.pallas import tpu as pltpu
from jax.sharding import PartitionSpec as P

EPS = 1e-06
NEG = -1000000000.0
LIMITS = (12, 16, 23, 32, 46, 64, 91)
HIGH = lax.Precision.HIGHEST
MESH = pl.DeviceIdType.MESH
BF = jnp.bfloat16
F32 = jnp.float32

GROUP = 8
LANES = 128
WIDE = 256
SLOTS = 5
OUTER_SPLIT = ((2, 1), (2, 1), (2, 1))
INNER_SPLIT = ((2, 2), (2, 2), (2, 2))
ATTN_SPLIT = (2, 1)
GROUP_SPLIT = ((2, 1), (2, 1), (2, 1))


def chunk_rows(row_share):
    rows = []
    for outer, inner in zip(OUTER_SPLIT, INNER_SPLIT):
        rows += [count * 2 * LANES for count in outer] + [count * 2 * row_share for count in inner]
    for split in (ATTN_SPLIT,) + GROUP_SPLIT:
        rows += [count * 2 * row_share for count in split]
    return rows


CHUNKS = len(chunk_rows(96))


def dot_nn(left, right):
    return jnp.dot(left, right, preferred_element_type=F32)


def dot_nt(left, right):
    return lax.dot_general(left, right, (((1,), (1,)), ((), ())), preferred_element_type=F32)


def dot_tn(left, right):
    return lax.dot_general(left, right, (((0,), (0,)), ((), ())), preferred_element_type=F32)


def buckets(relative):
    distance = jnp.abs(relative)
    far_bucket = 8 + sum(((distance >= thresh).astype(jnp.int32) for thresh in LIMITS))
    return jnp.where(relative > 0, 16, 0) + jnp.where(distance < 8, distance, far_bucket)


def loop(count, body):
    lax.fori_loop(0, count, lambda index, none: (body(index), none)[1], None)


def at(index, size):
    if isinstance(index, int):
        return pl.ds(index * size, size)
    return pl.ds(pl.multiple_of(index * size, size), size)


def layer_kernel(
    lo_count,
    hidden,
    cot,
    query_len,
    doc_len,
    wq_hbm,
    wk_hbm,
    wv_hbm,
    wo_hbm,
    w1_hbm,
    w2_hbm,
    gain1_hbm,
    gain2_hbm,
    table_hbm,
    layer_out,
    grad_in,
    shares,
    small_out,
    x_row,
    c_row,
    wq,
    wk,
    wv,
    wo,
    w1,
    w2,
    n1,
    q,
    k,
    v,
    probs,
    o,
    n2,
    gain1,
    gain2,
    table,
    z_turned,
    turned,
    mid,
    acc_b,
    z,
    du,
    bias,
    vec,
    sums,
    d_three,
    dsc,
    tacc,
    grads,
    r_core,
    r_first,
    r_second,
    z_end,
    z_mid,
    small,
    small_in,
    w_sem,
    own_sem,
    x_send,
    x_recv,
    c_send,
    c_recv,
    y_send,
    y_recv,
    i_send,
    i_recv,
    core_send,
    core_recv,
    first_send,
    first_recv,
    second_send,
    second_recv,
    end_send,
    end_recv,
    mid_send,
    mid_recv,
    back_send,
    back_recv,
    share_sem,
    small_send,
    small_recv,
):
    dp = lax.axis_index("dp")
    sq = lax.axis_index("seq")
    seq_count, block, width = hidden.shape
    length = x_row.shape[0]
    heads, bucket_count = table.shape
    pairs = heads // 2
    head_group = WIDE // LANES
    row_share = width // GROUP
    parts = w1_hbm.shape[1] // (GROUP * LANES)
    part_cols = GROUP * LANES
    vec_len = vec.shape[1]

    high = dp // lo_count
    bit0 = lax.rem(high, 2)
    bit1 = lax.rem(high // 2, 2)
    bit2 = lax.rem(high // 4, 2)
    step1 = 2 * lo_count * (1 - 2 * bit1)
    step2 = 4 * lo_count * (1 - 2 * bit2)
    core_dev = (dp + lo_count * (1 - 2 * bit0), sq)
    first_dev = (dp + (1 - bit0) * step1 + bit0 * step2, sq)
    second_dev = (dp + bit0 * step1 + (1 - bit0) * step2, sq)
    first_bit = (1 - bit0) * bit1 + bit0 * bit2
    second_bit = (1 - bit0) * bit2 + bit0 * bit1
    pair_dev = (dp, sq + 1 - 2 * lax.rem(sq, 2))
    mid_dev = (dp, 3 - sq)
    is_end = jnp.logical_or(sq == 0, sq == seq_count - 1)
    is_mid = jnp.logical_not(is_end)
    row_devs = [lax.rem(sq + step, seq_count) for step in range(1, seq_count)]

    def remote(src, dst, send, recv, device):
        return pltpu.make_async_remote_copy(
            src_ref=src, dst_ref=dst, send_sem=send, recv_sem=recv, device_id=device, device_id_type=MESH
        )

    barrier = pltpu.get_barrier_semaphore()
    for device in [core_dev, first_dev, second_dev] + [(dp, other) for other in row_devs]:
        pl.semaphore_signal(barrier, inc=1, device_id=device, device_id_type=MESH)
    pl.semaphore_wait(barrier, 3 + len(row_devs))

    def deal(src_of, dst_of, send, recv):
        def copy(index):
            other = row_devs[index]
            return remote(src_of(other), dst_of(sq), send.at[index], recv.at[sq], (dp, other))

        def start(index):
            copy(index).start()

        def arrived(other):
            remote(src_of(other), dst_of(other), send.at[0], recv.at[other], (dp, other)).wait_recv()

        def sent():
            for index in range(len(row_devs)):
                copy(index).wait_send()

        return start, arrived, sent

    x_start, x_arrived, x_sent = deal(
        lambda other: hidden.at[other], lambda src: x_row.at[at(src, block)], x_send, x_recv
    )
    c_start, c_arrived, c_sent = deal(
        lambda other: cot.at[other], lambda src: c_row.at[at(src, block)], c_send, c_recv
    )
    y_start, y_arrived, y_sent = deal(
        lambda other: dsc.at[at(other, block), pl.ds(0, width)], lambda src: layer_out.at[src], y_send, y_recv
    )
    i_start, i_arrived, i_sent = deal(
        lambda other: n2.at[at(other, block)], lambda src: grad_in.at[src], i_send, i_recv
    )
    own_x = pltpu.make_async_copy(hidden.at[sq], x_row.at[at(sq, block)], own_sem.at[0])
    own_c = pltpu.make_async_copy(cot.at[sq], c_row.at[at(sq, block)], own_sem.at[1])
    own_y = pltpu.make_async_copy(dsc.at[at(sq, block), pl.ds(0, width)], layer_out.at[sq], own_sem.at[2])
    own_i = pltpu.make_async_copy(n2.at[at(sq, block)], grad_in.at[sq], own_sem.at[3])

    for index in range(len(row_devs)):
        x_start(index)
    own_x.start()
    params = [
        pltpu.make_async_copy(src, dst, own_sem.at[4 + index])
        for index, (src, dst) in enumerate(((gain1_hbm, gain1), (gain2_hbm, gain2), (table_hbm, table)))
    ]
    for copy in params:
        copy.start()
    square = [
        pltpu.make_async_copy(src, dst, w_sem.at[index])
        for index, (src, dst) in enumerate(((wq_hbm, wq), (wk_hbm, wk), (wv_hbm, wv), (wo_hbm, wo)))
    ]
    for copy in square:
        copy.start()

    def part_copies(part):
        span = parts * LANES
        copies = []
        for share in range(GROUP):
            place = pl.ds(share * span + part * LANES, LANES)
            cols = pl.ds(share * LANES, LANES)
            copies.append(pltpu.make_async_copy(w1_hbm.at[:, place], w1.at[part, :, cols], w_sem.at[4 + 2 * part]))
            copies.append(pltpu.make_async_copy(w2_hbm.at[place], w2.at[part, cols], w_sem.at[5 + 2 * part]))
        return copies

    def part_wait(part):
        pltpu.make_async_copy(w1.at[part], w1.at[part], w_sem.at[4 + 2 * part]).wait()
        pltpu.make_async_copy(w2.at[part], w2.at[part], w_sem.at[5 + 2 * part]).wait()

    for part in range(parts):
        for copy in part_copies(part):
            copy.start()
    own_c.start()

    sizes = chunk_rows(row_share)

    def span(chunk):
        return pl.ds(sum(sizes[:chunk]), sizes[chunk])

    def piece(ref, chunk, *index):
        lead = index + (slice(None),) * (len(ref.shape) - 2 - len(index))
        return ref.at[lead + (span(chunk),)]

    def grad_half(chunk, side):
        return grads.at[chunk % SLOTS, side, :, :, pl.ds(0, sizes[chunk])]

    def core_copy(chunk):
        return remote(
            grad_half(chunk, 1 - bit0), piece(r_core, chunk), core_send.at[chunk], core_recv.at[chunk], core_dev
        )

    def first_copy(chunk):
        return remote(
            piece(r_core, chunk, 1 - first_bit),
            piece(r_first, chunk),
            first_send.at[chunk],
            first_recv.at[chunk],
            first_dev,
        )

    def second_copy(chunk):
        return remote(
            piece(r_first, chunk, 1 - second_bit),
            piece(r_second, chunk),
            second_send.at[chunk],
            second_recv.at[chunk],
            second_dev,
        )

    def end_copy(chunk):
        return remote(
            piece(r_second, chunk), piece(z_end, chunk), end_send.at[chunk], end_recv.at[chunk], pair_dev
        )

    def mid_copy(chunk):
        return remote(
            piece(r_second, chunk), piece(z_mid, chunk), mid_send.at[chunk], mid_recv.at[chunk], mid_dev
        )

    def back_copy(chunk):
        return remote(
            piece(z_end, chunk), piece(shares, chunk), back_send.at[chunk], back_recv.at[chunk], pair_dev
        )

    def share_copy(chunk):
        return pltpu.make_async_copy(piece(z_end, chunk), piece(shares, chunk), share_sem.at[chunk])

    def core_done(chunk):
        copy = core_copy(chunk)
        copy.wait_recv()
        for one in range(2):
            for two in range(2):
                r_core[one, two, span(chunk)] += grads[chunk % SLOTS, bit0, one, two, pl.ds(0, sizes[chunk])]
        first_copy(chunk).start()
        copy.wait_send()

    def first_done(chunk):
        first_copy(chunk).wait_recv()
        for one in range(2):
            r_first[one, span(chunk)] += r_core[first_bit, one, span(chunk)]
        second_copy(chunk).start()

    def second_done(chunk):
        second_copy(chunk).wait_recv()
        r_second[span(chunk)] += r_first[second_bit, span(chunk)]

        @pl.when(is_end)
        def _():
            end_copy(chunk).start()

    def end_done(chunk):
        @pl.when(is_mid)
        def _():
            end_copy(chunk).wait_recv()
            r_second[span(chunk)] += z_end[span(chunk)]
            mid_copy(chunk).start()

    def mid_done(chunk):
        @pl.when(is_mid)
        def _():
            mid_copy(chunk).wait_recv()
            z_end[span(chunk)] = r_second[span(chunk)] + z_mid[span(chunk)]
            back_copy(chunk).start()
            share_copy(chunk).start()

    def back_done(chunk):
        @pl.when(is_end)
        def _():
            back_copy(chunk).wait_recv()

    stages = (core_done, first_done, second_done, end_done, mid_done, back_done)

    def settle():
        for chunk in range(CHUNKS):
            first_copy(chunk).wait_send()
            second_copy(chunk).wait_send()

        @pl.when(is_end)
        def _():
            for chunk in range(CHUNKS):
                end_copy(chunk).wait_send()

        @pl.when(is_mid)
        def _():
            for chunk in range(CHUNKS):
                mid_copy(chunk).wait_send()
                back_copy(chunk).wait_send()
                share_copy(chunk).wait()

    def small_copy(step):
        device = (core_dev, (dp + step1, sq), (dp + step2, sq), pair_dev, (dp, lax.rem(sq + 2, 4)))[step]
        return remote(small.at[step], small_in.at[step], small_send.at[step], small_recv.at[step], device)

    def small_done(step):
        small_copy(step).wait_recv()
        if step < 4:
            small[step + 1] = small[step] + small_in[step]
            small_copy(step + 1).start()
        else:
            small_out[...] = small[step] + small_in[step]

    def tick(spot):
        for what, index in PLAN.get(spot, ()):
            if what == "y":
                y_start(index)
            elif what == "i":
                i_start(index)
            elif what == "s":
                small_done(index)
            else:
                stages[what](index)

    def tiles(split, first, kind, part, body):
        done = 0
        for place, count in enumerate(split):
            chunk = first + place
            if count == 1:
                body(chunk, done, 0)
            else:
                loop(count, lambda index: body(chunk, done + index, index))
            core_copy(chunk).start()
            tick((kind, part, place))
            done += count
        return first + len(split)

    def place_of(share):
        one, two, three = share % 2, (share // 2) % 2, share // 4
        return (one, two, three) if one == 0 else (one, three, two)

    for copy in params:
        copy.wait()
    distance = lax.broadcasted_iota(jnp.int32, (1, vec_len), 1) - vec_len // 2
    bucket_row = buckets(distance)
    one_hot = (
        jnp.broadcast_to(bucket_row, (bucket_count, vec_len))
        == lax.broadcasted_iota(jnp.int32, (bucket_count, vec_len), 0)
    ).astype(F32)
    vec[pl.ds(0, heads), :] = dot_nn(table[...], one_hot.astype(BF))
    sub = lax.broadcasted_iota(jnp.int32, (8, vec_len), 0)

    def build_bias(head):
        rows = jnp.broadcast_to(vec[pl.ds(head, 1), :], (8, vec_len))
        for shift in (1, 2, 4):
            rows = jnp.where((sub & shift) != 0, pltpu.roll(rows, shift, 1), rows)
        shift = 8
        while shift < block:
            rows = jnp.concatenate([rows, pltpu.roll(rows, shift, 1)], axis=0)
            shift *= 2
        bias[head] = rows.astype(BF)

    loop(heads, build_bias)

    total_len = query_len[sq] + doc_len[sq]
    key_mask = jnp.where(
        lax.broadcasted_iota(jnp.int32, (1, length), 1) < total_len, jnp.float32(0), jnp.float32(NEG)
    )
    low_lanes = lax.broadcasted_iota(jnp.int32, (1, LANES), 1) < LANES // 2

    def half_of(values, half):
        keep = low_lanes if half == 0 else jnp.logical_not(low_lanes)
        return jnp.where(keep, values, jnp.zeros_like(values))

    gain_one = gain1[...].astype(F32).reshape(1, width)
    gain_two = gain2[...].astype(F32).reshape(1, width)

    own_x.wait()
    for other in row_devs:
        x_arrived(other)
    for index in range(len(row_devs)):
        c_start(index)

    def norm_first(index):
        rows = at(index, block)
        values = x_row[rows, :].astype(F32)
        factor = lax.rsqrt(jnp.mean(values * values, axis=-1, keepdims=True) + EPS)
        n1[rows, :] = (values * factor * gain_one).astype(BF)

    loop(seq_count, norm_first)
    for copy in square:
        copy.wait()

    def project(index):
        cols = at(index, WIDE)
        q[:, cols] = dot_nn(n1[...], wq[:, cols]).astype(BF)
        k[:, cols] = dot_nn(n1[...], wk[:, cols]).astype(BF)
        v[:, cols] = dot_nn(n1[...], wv[:, cols]).astype(BF)

    loop(width // WIDE, project)

    def attend(pair):
        cols = at(pair, LANES)
        keys = k[:, cols]
        values = v[:, cols]
        for tile in range(length // WIDE):
            rows = pl.ds(tile * WIDE, WIDE)
            queries = q[rows, cols]
            total = None
            for half in range(2):
                head = 2 * pair + half
                scores = dot_nt(half_of(queries, half), keys)
                weights = []
                for part in range(WIDE // block):
                    start = vec_len // 2 - tile * WIDE - part * block
                    here = scores[part * block : (part + 1) * block]
                    here = here + bias[head, :, pl.ds(start, length)].astype(F32) + key_mask
                    here = jnp.exp(here - jnp.max(here, axis=-1, keepdims=True))
                    scale = 1.0 / jnp.sum(here, axis=-1, keepdims=True)
                    weights.append((here * scale).astype(BF))
                weights = jnp.concatenate(weights, axis=0)
                probs[head, rows, :] = weights
                term = dot_nn(weights, half_of(values, half))
                total = term if total is None else total + term
            o[rows, cols] = total.astype(BF)

    loop(pairs, attend)

    def attn_out(index):
        cols = at(index, WIDE)
        mid[:, cols] = x_row[:, cols].astype(F32) + dot_nn(o[...], wo[:, cols])

    loop(width // WIDE, attn_out)

    def norm_second(index):
        rows = at(index, block)
        values = mid[rows, :]
        factor = lax.rsqrt(jnp.mean(values * values, axis=-1, keepdims=True) + EPS)
        n2[rows, :] = (values * factor * gain_two).astype(BF)

    loop(seq_count, norm_second)

    def turn(source):
        def body(index):
            span = at(index, LANES)
            turned[span, :] = source[:, span].T

        loop(width // LANES, body)

    def put(chunk, values, tile):
        rows = values.shape[0] // GROUP
        for share in range(GROUP):
            for side in range(2):
                one, two, three = place_of(share)
                place = (2 * tile + side) * rows
                if not isinstance(tile, int):
                    place = pl.multiple_of(place, rows)
                grads[chunk % SLOTS, one, two, three, pl.ds(place, rows), :] = values[
                    share * rows : (share + 1) * rows, side * LANES : (side + 1) * LANES
                ].astype(BF)

    row_blocks = length // block
    for part in range(parts):
        part_wait(part)

        def forward(index):
            cols = at(index, WIDE)
            inner = dot_nn(n2[...], w1[part, :, cols])
            square_in = inner * inner
            bend = jnp.tanh(inner * (0.7978845608028654 + (0.7978845608028654 * 0.044715) * square_in))
            half_in = 0.5 * inner
            z[part, :, cols] = (half_in + half_in * bend).astype(BF)
            slope = 0.7978845608028654 + (3 * 0.7978845608028654 * 0.044715) * square_in
            slope = (0.5 + 0.5 * bend + half_in * (1 - bend * bend) * slope).astype(BF)
            for rows in range(row_blocks):
                bias[part * row_blocks + rows, :, cols] = slope[rows * block : (rows + 1) * block]

        loop(part_cols // WIDE, forward)

    def layer_tile(index):
        cols = at(index, WIDE)
        total = mid[:, cols]
        for part in range(parts):
            total = total + dot_nn(z[part], w2[part, :, cols])
        dsc[:, cols] = total.astype(BF)

    loop(width // WIDE, layer_tile)
    own_y.start()
    tick(("y", 0, 0))
    turn(n2)
    own_c.wait()
    for other in row_devs:
        c_arrived(other)

    chunk = 0
    for part in range(parts):

        def backward(index):
            cols = at(index, WIDE)
            back = dot_nt(c_row[...], w2[part, cols, :])
            for rows in range(row_blocks):
                span_rows = pl.ds(rows * block, block)
                slope = bias[part * row_blocks + rows, :, cols].astype(F32)
                du[span_rows, cols] = (back[rows * block : (rows + 1) * block] * slope).astype(BF)
            z_turned[cols, :] = z[part, :, cols].T

        loop(part_cols // WIDE, backward)
        tick(("u", part, 0))

        def outer_tile(chunk, tile, place):
            put(chunk, dot_nn(z_turned[...], c_row[:, at(tile, WIDE)]), place)

        chunk = tiles(OUTER_SPLIT[part], chunk, "o", part, outer_tile)

        def inner_tile(chunk, tile, place):
            put(chunk, dot_nn(turned[...], du[:, at(tile, WIDE)]), place)

        chunk = tiles(INNER_SPLIT[part], chunk, "n", part, inner_tile)

        def add_up(index):
            cols = at(index, WIDE)
            back = dot_nt(du[...], w1[part, cols, :])
            if part == 0:
                acc_b[:, cols] = back
            else:
                acc_b[:, cols] += back

        loop(width // WIDE, add_up)
        tick(("s", part, 0))

    sums[...] = jnp.zeros_like(sums)

    def back_second(index):
        rows = at(index, block)
        values = mid[rows, :]
        back = acc_b[rows, :]
        factor = lax.rsqrt(jnp.mean(values * values, axis=-1, keepdims=True) + EPS)
        sums[1:2, :] += jnp.sum(back * values * factor, axis=0, keepdims=True)
        scaled = back * gain_two
        inside = jnp.mean(scaled * values, axis=-1, keepdims=True)
        total = c_row[rows, :].astype(F32) + factor * scaled - values * (factor * factor * factor * inside)
        acc_b[rows, :] = total
        n2[rows, :] = total.astype(BF)

    loop(seq_count, back_second)
    turn(o)
    tick(("r", 0, 0))

    def attn_out_tile(chunk, tile, place):
        cols = at(tile, WIDE)
        put(chunk, dot_nn(turned[...], n2[:, cols]), place)
        c_row[:, cols] = dot_nt(n2[...], wo[cols, :]).astype(BF)

    chunk = tiles(ATTN_SPLIT, chunk, "a", 0, attn_out_tile)
    turn(n1)

    def attend_back(group, inside):
        pair = group * head_group + inside
        cols = at(pair, LANES)
        keys = k[:, cols]
        values = v[:, cols]
        queries = q[:, cols]
        backs = c_row[:, cols]
        product = backs.astype(F32) * o[:, cols].astype(F32)
        for half in range(2):
            head = 2 * pair + half
            dot_sum = jnp.sum(half_of(product, half), axis=-1, keepdims=True)
            tacc[...] = jnp.zeros_like(tacc)
            for tile in range(length // WIDE):
                rows = pl.ds(tile * WIDE, WIDE)
                back = dot_nt(half_of(backs[tile * WIDE : (tile + 1) * WIDE], half), values)
                for part in range(WIDE // block):
                    base = tile * WIDE + part * block
                    start = vec_len // 2 - base
                    score = probs[head, pl.ds(base, block), :].astype(F32) * (
                        back[part * block : (part + 1) * block] - dot_sum[base : base + block]
                    )
                    tacc[:, pl.ds(start, length)] += score
                    dsc[pl.ds(base, block), pl.ds(half * length, length)] = score.astype(BF)
            rows = tacc[...]
            size = block
            while size > 8:
                size //= 2
                rows = rows[:size] + pltpu.roll(rows[size:], vec_len - size, 1)
            for shift in (4, 2, 1):
                rows = jnp.where((sub & shift) != 0, pltpu.roll(rows, vec_len - shift, 1), rows)
            vec[pl.ds(head, 1), :] = jnp.sum(rows, axis=0, keepdims=True)
        out = at(inside, LANES)
        d_three[0, :, out] = (
            dot_nn(dsc[:, pl.ds(0, length)], half_of(keys, 0)) + dot_nn(dsc[:, pl.ds(length, length)], half_of(keys, 1))
        ).astype(BF)
        d_three[1, :, out] = (
            dot_tn(dsc[:, pl.ds(0, length)], half_of(queries, 0)) + dot_tn(dsc[:, pl.ds(length, length)], half_of(queries, 1))
        ).astype(BF)
        d_three[2, :, out] = (
            dot_tn(probs[2 * pair], half_of(backs, 0)) + dot_tn(probs[2 * pair + 1], half_of(backs, 1))
        ).astype(BF)

    own_y.wait()
    y_sent()
    for group in range(width // WIDE):
        for inside in range(head_group):
            attend_back(group, inside)
            tick(("h", head_group * group + inside, 0))

        def group_tile(chunk, tile, place):
            put(chunk, dot_nn(turned[...], d_three[tile]), place)

        chunk = tiles(GROUP_SPLIT[group], chunk, "g", group, group_tile)
        cols = pl.ds(group * WIDE, WIDE)
        term = dot_nt(d_three[0], wq[:, cols]) + dot_nt(d_three[1], wk[:, cols]) + dot_nt(d_three[2], wv[:, cols])
        if group == 0:
            mid[...] = term
        else:
            mid[...] += term
        tick(("d", group, 0))

    def back_first(index):
        rows = at(index, block)
        values = x_row[rows, :].astype(F32)
        back = mid[rows, :]
        factor = lax.rsqrt(jnp.mean(values * values, axis=-1, keepdims=True) + EPS)
        sums[0:1, :] += jnp.sum(back * values * factor, axis=0, keepdims=True)
        scaled = back * gain_one
        inside = jnp.mean(scaled * values, axis=-1, keepdims=True)
        total = acc_b[rows, :] + factor * scaled - values * (factor * factor * factor * inside)
        n2[rows, :] = total.astype(BF)

    loop(seq_count, back_first)
    table_sum = lax.dot_general(
        vec[pl.ds(0, heads), :],
        one_hot,
        (((1,), (1,)), ((), ())),
        precision=HIGH,
        preferred_element_type=F32,
    )
    small[0] = jnp.zeros(small.shape[1:], F32)
    for share in range(GROUP):
        own = pl.ds(share, 1)
        small[0, own, pl.ds(0, row_share)] = sums[0:1, share * row_share : (share + 1) * row_share]
        small[0, own, pl.ds(LANES, row_share)] = sums[1:2, share * row_share : (share + 1) * row_share]
    small[0, pl.ds(8, heads), pl.ds(0, bucket_count)] = table_sum
    small_copy(0).start()
    own_i.start()
    tick(("e", 0, 0))
    for step in range(5):
        small_copy(step).wait_send()
    settle()
    own_i.wait()
    for other in row_devs:
        y_arrived(other)
        i_arrived(other)
    x_sent()
    c_sent()
    i_sent()


PLAN = {
    ("y", 0, 0): (("y", 0),),
    ("u", 0, 0): (("y", 1),),
    ("o", 0, 1): (("y", 2),),
    ("n", 0, 1): ((0, 0), (0, 1)),
    ("s", 0, 0): ((0, 2),),
    ("u", 1, 0): ((0, 3),),
    ("o", 1, 1): ((1, 0),),
    ("n", 1, 0): ((1, 1),),
    ("n", 1, 1): ((0, 4), (0, 5)),
    ("s", 1, 0): ((2, 0), (1, 2)),
    ("u", 2, 0): ((0, 6), (0, 7), (1, 3)),
    ("o", 2, 0): ((2, 1),),
    ("o", 2, 1): ((2, 2),),
    ("n", 2, 1): ((1, 4), (0, 8)),
    ("s", 2, 0): ((0, 9), (2, 3)),
    ("r", 0, 0): ((1, 5), (0, 10)),
    ("a", 0, 0): ((2, 4), (3, 0), (1, 6)),
    ("a", 0, 1): ((2, 5),),
    ("h", 0, 0): ((3, 2), (1, 7)),
    ("h", 1, 0): ((4, 0), (3, 1), (3, 3), (2, 6), (1, 8), (0, 11), (0, 12), (2, 7), (0, 13)),
    ("g", 0, 0): ((4, 1), (4, 2), (1, 9), (5, 1)),
    ("d", 0, 0): ((5, 0),),
    ("h", 2, 0): ((3, 4), (1, 10), (4, 3), (3, 5), (2, 8)),
    ("h", 3, 0): ((2, 9), (1, 11), (5, 2), (0, 14), (0, 15)),
    ("g", 1, 0): ((5, 3), (3, 6), (1, 12)),
    ("g", 1, 1): ((4, 4), (3, 7), (2, 10), (4, 5), (1, 13), (5, 5), (0, 16)),
    ("d", 1, 0): ((2, 11),),
    ("h", 4, 0): ((4, 6), (2, 12), (1, 14), (0, 17)),
    ("h", 5, 0): ((5, 4), (4, 7), (3, 8), (3, 9), (1, 15), (2, 13)),
    ("g", 2, 0): ((5, 6), (2, 14), (1, 16)),
    ("g", 2, 1): ((3, 10), (1, 17), (5, 7), (2, 15)),
    ("e", 0, 0): ((3, 11), (0, 18), (3, 12), (2, 17), (2, 16), (4, 8), (4, 9), (0, 19), ("i", 0), ("s", 0), (4, 10), (1, 18), (1, 19), (3, 13), (4, 11), (3, 14), (5, 11), (2, 18), (5, 8), ("s", 1), (5, 9), (3, 15), (4, 12), (2, 19), ("s", 2), ("i", 1), (4, 15), (3, 16), (3, 17), (4, 13), (5, 12), (5, 10), ("s", 3), (4, 14), (3, 18), (5, 13), (3, 19), ("i", 2), (4, 16), (4, 17), (5, 15), ("s", 4), (5, 16), (5, 17), (4, 18), (5, 14), (4, 19), (5, 18), (5, 19)),
}


def unpack_kernel(parts, row_share, shares_hbm, small_hbm, layer_in, grad_in_in, *refs):
    outs, held, (shares, small, through, sems, in_sems) = refs[:11], refs[11:20], refs[20:]
    moves = [pltpu.make_async_copy(through.at[index], outs[index], sems.at[index]) for index in range(2)]
    loads = [
        pltpu.make_async_copy(src, dst, in_sems.at[index])
        for index, (src, dst) in enumerate(
            ((shares_hbm, shares), (small_hbm, small), (layer_in, through.at[0]), (grad_in_in, through.at[1]))
        )
    ]
    for copy in loads:
        copy.start()
    for copy in loads[:2]:
        copy.wait()
    gq, gk, gv, go, gi, gf, gain_a, gain_f, table = held
    blocks = gq.shape[1] // LANES
    part_rows = blocks * LANES + GROUP * row_share

    def take(start, rows):
        return shares[pl.ds(start, rows), :].astype(F32)

    def give(index):
        moves.append(pltpu.make_async_copy(held[index], outs[2 + index], sems.at[2 + index]))
        moves[-1].start()

    for part in range(parts):
        for col in range(blocks):
            gf[pl.ds(part * LANES, LANES), pl.ds(col * LANES, LANES)] = take(part * part_rows + col * LANES, LANES)
    give(5)
    for part in range(parts):
        base = part * part_rows + blocks * LANES
        for share in range(GROUP):
            gi[:, pl.ds((share * parts + part) * LANES, LANES)] = take(base + share * row_share, row_share)
    give(4)
    base = parts * part_rows
    for col in range(blocks):
        go[:, pl.ds(col * LANES, LANES)] = take(base + col * row_share, row_share)
    give(3)
    for index, ref in enumerate((gq, gk, gv)):
        for group in range(blocks // 2):
            for side in range(2):
                place = base + (1 + group) * blocks * row_share + (2 * index + side) * row_share
                ref[:, pl.ds(group * WIDE + side * LANES, LANES)] = take(place, row_share)
        give(index)
    own = lax.broadcasted_iota(jnp.int32, (GROUP, row_share), 0) == lax.axis_index("dp") % GROUP
    for first, ref in ((0, gain_a), (LANES, gain_f)):
        ref[...] = jnp.sum(jnp.where(own, small[pl.ds(0, GROUP), pl.ds(first, row_share)], 0.0), axis=0)
    table[...] = small[pl.ds(8, table.shape[0]), pl.ds(0, table.shape[1])]
    for index in (6, 7, 8):
        give(index)
    for index in range(2):
        loads[2 + index].wait()
        moves[index].start()
    for copy in moves:
        copy.wait()


def on_device(
    dp_count,
    hidden_in,
    query_lengths,
    doc_lengths,
    w_query,
    w_key,
    w_value,
    w_attn_out,
    w_inner,
    w_outer,
    gain_attn,
    gain_ffn,
    bias_table,
    cotangent,
):
    rows, block, width = hidden_in.shape
    length = rows * block
    bucket_count, heads = bias_table.shape
    ffn = w_inner.shape[1]
    part_cols = GROUP * LANES
    parts = ffn // part_cols
    vec_len = 2 * length
    lo_count = dp_count // GROUP
    row_share = width // GROUP

    def vm(*shape, dtype=BF):
        return pltpu.VMEM(shape, dtype)

    def dma(count):
        return pltpu.SemaphoreType.DMA((count,))

    hbm = pl.BlockSpec(memory_space=pl.ANY)
    vmem = pl.BlockSpec(memory_space=pltpu.VMEM)
    smem = pl.BlockSpec(memory_space=pltpu.SMEM)
    small_rows = 8 + heads
    small_cols = 2 * LANES
    total_rows = sum(chunk_rows(row_share))
    layer_raw, grad_raw, shares, small = pl.pallas_call(
        partial(layer_kernel, lo_count),
        out_shape=(
            jax.ShapeDtypeStruct(hidden_in.shape, BF),
            jax.ShapeDtypeStruct(hidden_in.shape, BF),
            jax.ShapeDtypeStruct((total_rows, LANES), BF),
            jax.ShapeDtypeStruct((small_rows, small_cols), F32),
        ),
        in_specs=[hbm, hbm, smem, smem] + [hbm] * 9,
        out_specs=(hbm, hbm, hbm, vmem),
        scratch_shapes=[
            vm(length, width),
            vm(length, width),
            vm(width, width),
            vm(width, width),
            vm(width, width),
            vm(width, width),
            vm(parts, width, part_cols),
            vm(parts, part_cols, width),
            vm(length, width),
            vm(length, width),
            vm(length, width),
            vm(length, width),
            vm(heads, length, length),
            vm(length, width),
            vm(length, width),
            vm(width),
            vm(width),
            vm(heads, bucket_count),
            vm(part_cols, length),
            vm(width, length),
            vm(length, width, dtype=F32),
            vm(length, width, dtype=F32),
            vm(parts, length, part_cols),
            vm(length, part_cols),
            vm(heads, block, vec_len),
            vm(16, vec_len, dtype=F32),
            vm(8, width, dtype=F32),
            vm(3, length, WIDE),
            vm(length, 2 * length),
            vm(block, vec_len, dtype=F32),
            vm(SLOTS, 2, 2, 2, max(chunk_rows(row_share)), LANES),
            vm(2, 2, total_rows, LANES),
            vm(2, total_rows, LANES),
            vm(total_rows, LANES),
            vm(total_rows, LANES),
            vm(total_rows, LANES),
            vm(5, small_rows, small_cols, dtype=F32),
            vm(5, small_rows, small_cols, dtype=F32),
            dma(4 + 2 * parts),
            dma(7),
        ]
        + [dma(rows)] * 8
        + [dma(CHUNKS)] * 13
        + [dma(5)] * 2,
        compiler_params=pltpu.CompilerParams(
            collective_id=0, has_side_effects=True, vmem_limit_bytes=64 * 2**20 - 2**19
        ),
    )(
        hidden_in,
        cotangent,
        query_lengths,
        doc_lengths,
        w_query,
        w_key,
        w_value,
        w_attn_out,
        w_inner,
        w_outer,
        gain_attn,
        gain_ffn,
        bias_table.T,
    )
    grad_shapes = [(row_share, width)] * 4 + [(row_share, ffn), (ffn // GROUP, width), (row_share,), (row_share,)]
    grad_shapes.append((heads, bucket_count))
    layer_out, grad_in, *grads = pl.pallas_call(
        partial(unpack_kernel, parts, row_share),
        out_shape=[jax.ShapeDtypeStruct(hidden_in.shape, BF)] * 2
        + [jax.ShapeDtypeStruct(shape, F32) for shape in grad_shapes],
        in_specs=[hbm] * 4,
        out_specs=[hbm] * 11,
        scratch_shapes=[vm(*shape, dtype=F32) for shape in grad_shapes]
        + [vm(total_rows, LANES), vm(small_rows, small_cols, dtype=F32), vm(2, *hidden_in.shape), dma(11), dma(4)],
        compiler_params=pltpu.CompilerParams(vmem_limit_bytes=64 * 2**20 - 2**19),
    )(shares, small, layer_raw, grad_raw)
    if lo_count > 1:
        high = lax.axis_index("dp") // lo_count

        def spread(part):
            whole = jnp.zeros((GROUP,) + part.shape, F32)
            whole = lax.dynamic_update_index_in_dim(whole, part, high, 0)
            whole = whole.reshape((GROUP * part.shape[0],) + part.shape[1:])
            return lax.psum_scatter(whole, "dp", scatter_dimension=0, tiled=True)

        small = lax.psum(small, "dp") / GROUP
        gain_rows = width // dp_count
        start = lax.axis_index("dp") * gain_rows
        gains = [
            lax.dynamic_slice_in_dim(small[:GROUP, first : first + row_share].reshape(width), start, gain_rows)
            for first in (0, LANES)
        ]
        grads = [spread(part) for part in grads[:6]] + gains + [small[8 : 8 + heads, :bucket_count]]
    return (layer_out, grad_in, *grads[:8], grads[8].T)


def solution(mesh):
    return jax.shard_map(
        partial(on_device, mesh.shape["dp"]),
        mesh=mesh,
        in_specs=(
            P("dp", "seq", None),
            P("dp"),
            P("dp"),
            P(),
            P(),
            P(),
            P(),
            P(),
            P(),
            P(),
            P(),
            P(),
            P("dp", "seq", None),
        ),
        out_specs=(
            P("dp", "seq", None),
            P("dp", "seq", None),
            P("dp", None),
            P("dp", None),
            P("dp", None),
            P("dp", None),
            P("dp", None),
            P("dp", None),
            P("dp"),
            P("dp"),
            P(),
        ),
        check_vma=False,
    )
```

profile of v0, /device:TPU:0, one launch (start us, length us, event | category | flops | bytes accessed | tf_op | source)
XLA Modules:
  0.0 154.4 jit_solution(14927325653545099883)
XLA Ops:
  0.6 149.5 %shard_map.212 = (bf16[4,128,768]{2,1,0:T(8,128)(2,1)}, bf16[4,128,768]{2,1,0:T(8,128)(2,1)}, bf16[6912,128]{1,0:T(8,128)(2,1)}, f32[20,256]{1,0:T(8,128)}) custom-call(bf16[4,128,768]{2,1,0:T(8,128)(2,1)} %hidden.1, bf16[4,128,768]{2,1,0:T(8,128)(2,1)} %cot.1, s32[4]{0:T(128)} %query_len.1, s32[4]{0:T(128)} %doc_len.1, bf16[768,768]{1,0:T(8,128)(2,1)} %wq_hbm.1, ...), custom_call_target="tpu_custom_call" | custom-call | tf_op jit(solution)/shard_map/pallas_call | solution.py:860
  150.2 4.0 %shard_map.213 = (bf16[4,128,768]{2,1,0:T(8,128)(2,1)}, bf16[4,128,768]{2,1,0:T(8,128)(2,1)}, f32[96,768]{1,0:T(8,128)}, f32[96,768]{1,0:T(8,128)}, f32[96,768]{...) custom-call(bf16[6912,128]{1,0:T(8,128)(2,1)} %get-tuple-element.26., ...), custom_call_target="tpu_custom_call" | custom-call | tf_op jit(solution)/shard_map/pallas_call | solution.py:935
where the time goes:
time: 155 us; the launch traced here: 154 us
  Pallas kernels  154 us (99%)
    pallas_call x1, Pallas kernels, on_device(): pl.pallas_call(partial(layer_kernel, lo_count), out_shape=(jax.ShapeDtype...  150 us
    pallas_call x1, Pallas kernels, on_device(): pl.pallas_call(partial(unpack_kernel, parts, row_share), out_shape=[jax.S...  4.02 us

commit v1 on v0

--- a/solution.py
+++ b/solution.py
@@ -21,8 +21,8 @@
 SLOTS = 5
 OUTER_SPLIT = ((2, 1), (2, 1), (2, 1))
 INNER_SPLIT = ((2, 2), (2, 2), (2, 2))
-ATTN_SPLIT = (2, 1)
-GROUP_SPLIT = ((2, 1), (2, 1), (2, 1))
+ATTN_SPLIT = (3,)
+GROUP_SPLIT = ((3,), (3,), (2, 1))
 
 
 def chunk_rows(row_share):
@@ -111,7 +111,6 @@
     bias,
     vec,
     sums,
-    d_three,
     dsc,
     tacc,
     grads,
@@ -154,7 +153,6 @@
     length = x_row.shape[0]
     heads, bucket_count = table.shape
     pairs = heads // 2
-    head_group = WIDE // LANES
     row_share = width // GROUP
     parts = w1_hbm.shape[1] // (GROUP * LANES)
     part_cols = GROUP * LANES
@@ -214,12 +212,12 @@
         lambda other: dsc.at[at(other, block), pl.ds(0, width)], lambda src: layer_out.at[src], y_send, y_recv
     )
     i_start, i_arrived, i_sent = deal(
-        lambda other: n2.at[at(other, block)], lambda src: grad_in.at[src], i_send, i_recv
+        lambda other: du.at[at(other, block), pl.ds(0, width)], lambda src: grad_in.at[src], i_send, i_recv
     )
     own_x = pltpu.make_async_copy(hidden.at[sq], x_row.at[at(sq, block)], own_sem.at[0])
     own_c = pltpu.make_async_copy(cot.at[sq], c_row.at[at(sq, block)], own_sem.at[1])
     own_y = pltpu.make_async_copy(dsc.at[at(sq, block), pl.ds(0, width)], layer_out.at[sq], own_sem.at[2])
-    own_i = pltpu.make_async_copy(n2.at[at(sq, block)], grad_in.at[sq], own_sem.at[3])
+    own_i = pltpu.make_async_copy(du.at[at(sq, block), pl.ds(0, width)], grad_in.at[sq], own_sem.at[3])
 
     for index in range(len(row_devs)):
         x_start(index)
@@ -312,16 +310,22 @@
     def core_done(chunk):
         copy = core_copy(chunk)
         copy.wait_recv()
-        for one in range(2):
-            for two in range(2):
-                r_core[one, two, span(chunk)] += grads[chunk % SLOTS, bit0, one, two, pl.ds(0, sizes[chunk])]
+
+        def add(index):
+            one, two = index // 2, lax.rem(index, 2)
+            r_core[one, two, span(chunk)] += grads[chunk % SLOTS, bit0, one, two, pl.ds(0, sizes[chunk])]
+
+        loop(4, add)
         first_copy(chunk).start()
         copy.wait_send()
 
     def first_done(chunk):
         first_copy(chunk).wait_recv()
-        for one in range(2):
-            r_first[one, span(chunk)] += r_core[first_bit, one, span(chunk)]
+
+        def add(index):
+            r_first[index, span(chunk)] += r_core[first_bit, index, span(chunk)]
+
+        loop(2, add)
         second_copy(chunk).start()
 
     def second_done(chunk):
@@ -540,14 +544,19 @@
             inner = dot_nn(n2[...], w1[part, :, cols])
             square_in = inner * inner
             bend = jnp.tanh(inner * (0.7978845608028654 + (0.7978845608028654 * 0.044715) * square_in))
-            half_in = 0.5 * inner
-            z[part, :, cols] = (half_in + half_in * bend).astype(BF)
-            slope = 0.7978845608028654 + (3 * 0.7978845608028654 * 0.044715) * square_in
-            slope = (0.5 + 0.5 * bend + half_in * (1 - bend * bend) * slope).astype(BF)
+            gate = 0.5 + 0.5 * bend
+            active = inner * gate
+            z[part, :, cols] = active.astype(BF)
+            slope = 1.5957691216057308 + (6 * 0.7978845608028654 * 0.044715) * square_in
+            slope = (gate + active * ((1 - gate) * slope)).astype(BF)
             for rows in range(row_blocks):
                 bias[part * row_blocks + rows, :, cols] = slope[rows * block : (rows + 1) * block]
 
-        loop(part_cols // WIDE, forward)
+        def forward_two(index):
+            forward(2 * index)
+            forward(2 * index + 1)
+
+        loop(part_cols // (2 * WIDE), forward_two)
 
     def layer_tile(index):
         cols = at(index, WIDE)
@@ -615,19 +624,16 @@
         n2[rows, :] = total.astype(BF)
 
     loop(seq_count, back_second)
-    turn(o)
     tick(("r", 0, 0))
 
-    def attn_out_tile(chunk, tile, place):
-        cols = at(tile, WIDE)
-        put(chunk, dot_nn(turned[...], n2[:, cols]), place)
+    def back_out(index):
+        cols = at(index, WIDE)
         c_row[:, cols] = dot_nt(n2[...], wo[cols, :]).astype(BF)
 
-    chunk = tiles(ATTN_SPLIT, chunk, "a", 0, attn_out_tile)
-    turn(n1)
-
-    def attend_back(group, inside):
-        pair = group * head_group + inside
+    loop(width // WIDE, back_out)
+    tick(("r", 0, 1))
+
+    def attend_back(pair):
         cols = at(pair, LANES)
         keys = k[:, cols]
         values = v[:, cols]
@@ -657,35 +663,33 @@
             for shift in (4, 2, 1):
                 rows = jnp.where((sub & shift) != 0, pltpu.roll(rows, vec_len - shift, 1), rows)
             vec[pl.ds(head, 1), :] = jnp.sum(rows, axis=0, keepdims=True)
-        out = at(inside, LANES)
-        d_three[0, :, out] = (
+        z[0, :, cols] = (
             dot_nn(dsc[:, pl.ds(0, length)], half_of(keys, 0)) + dot_nn(dsc[:, pl.ds(length, length)], half_of(keys, 1))
         ).astype(BF)
-        d_three[1, :, out] = (
+        z[1, :, cols] = (
             dot_tn(dsc[:, pl.ds(0, length)], half_of(queries, 0)) + dot_tn(dsc[:, pl.ds(length, length)], half_of(queries, 1))
         ).astype(BF)
-        d_three[2, :, out] = (
+        z[2, :, cols] = (
             dot_tn(probs[2 * pair], half_of(backs, 0)) + dot_tn(probs[2 * pair + 1], half_of(backs, 1))
         ).astype(BF)
 
     own_y.wait()
     y_sent()
-    for group in range(width // WIDE):
-        for inside in range(head_group):
-            attend_back(group, inside)
-            tick(("h", head_group * group + inside, 0))
-
-        def group_tile(chunk, tile, place):
-            put(chunk, dot_nn(turned[...], d_three[tile]), place)
-
-        chunk = tiles(GROUP_SPLIT[group], chunk, "g", group, group_tile)
-        cols = pl.ds(group * WIDE, WIDE)
-        term = dot_nt(d_three[0], wq[:, cols]) + dot_nt(d_three[1], wk[:, cols]) + dot_nt(d_three[2], wv[:, cols])
-        if group == 0:
-            mid[...] = term
-        else:
-            mid[...] += term
-        tick(("d", group, 0))
+    for pair in range(pairs):
+        attend_back(pair)
+        tick(("h", pair, 0))
+
+    def back_project(index):
+        cols = at(index, WIDE)
+        span_cols = pl.ds(0, width)
+        mid[:, cols] = (
+            dot_nt(z[0, :, span_cols], wq[cols, :])
+            + dot_nt(z[1, :, span_cols], wk[cols, :])
+            + dot_nt(z[2, :, span_cols], wv[cols, :])
+        )
+
+    loop(width // WIDE, back_project)
+    tick(("d", 0, 0))
 
     def back_first(index):
         rows = at(index, block)
@@ -696,7 +700,7 @@
         scaled = back * gain_one
         inside = jnp.mean(scaled * values, axis=-1, keepdims=True)
         total = acc_b[rows, :] + factor * scaled - values * (factor * factor * factor * inside)
-        n2[rows, :] = total.astype(BF)
+        du[rows, pl.ds(0, width)] = total.astype(BF)
 
     loop(seq_count, back_first)
     table_sum = lax.dot_general(
@@ -714,6 +718,21 @@
     small[0, pl.ds(8, heads), pl.ds(0, bucket_count)] = table_sum
     small_copy(0).start()
     own_i.start()
+    tick(("i", 0, 0))
+
+    turn(o)
+
+    def attn_out_tile(chunk, tile, place):
+        put(chunk, dot_nn(turned[...], n2[:, at(tile, WIDE)]), place)
+
+    chunk = tiles(ATTN_SPLIT, chunk, "a", 0, attn_out_tile)
+    turn(n1)
+    for group in range(width // WIDE):
+
+        def group_tile(chunk, tile, place):
+            put(chunk, dot_nn(turned[...], z[tile, :, pl.ds(group * WIDE, WIDE)]), place)
+
+        chunk = tiles(GROUP_SPLIT[group], chunk, "g", group, group_tile)
     tick(("e", 0, 0))
     for step in range(5):
         small_copy(step).wait_send()
@@ -729,37 +748,31 @@
 
 PLAN = {
     ("y", 0, 0): (("y", 0),),
-    ("u", 0, 0): (("y", 1),),
-    ("o", 0, 1): (("y", 2),),
-    ("n", 0, 1): ((0, 0), (0, 1)),
-    ("s", 0, 0): ((0, 2),),
-    ("u", 1, 0): ((0, 3),),
-    ("o", 1, 1): ((1, 0),),
-    ("n", 1, 0): ((1, 1),),
-    ("n", 1, 1): ((0, 4), (0, 5)),
-    ("s", 1, 0): ((2, 0), (1, 2)),
-    ("u", 2, 0): ((0, 6), (0, 7), (1, 3)),
+    ("n", 0, 1): ((0, 0), ("y", 1)),
+    ("s", 0, 0): ((0, 1), (0, 2)),
+    ("o", 1, 1): (("y", 2),),
+    ("n", 1, 0): ((1, 0),),
+    ("n", 1, 1): ((1, 1),),
+    ("s", 1, 0): ((0, 3), (0, 4), (0, 5), (0, 6)),
+    ("u", 2, 0): ((2, 0), (1, 2)),
     ("o", 2, 0): ((2, 1),),
-    ("o", 2, 1): ((2, 2),),
-    ("n", 2, 1): ((1, 4), (0, 8)),
-    ("s", 2, 0): ((0, 9), (2, 3)),
-    ("r", 0, 0): ((1, 5), (0, 10)),
-    ("a", 0, 0): ((2, 4), (3, 0), (1, 6)),
-    ("a", 0, 1): ((2, 5),),
-    ("h", 0, 0): ((3, 2), (1, 7)),
-    ("h", 1, 0): ((4, 0), (3, 1), (3, 3), (2, 6), (1, 8), (0, 11), (0, 12), (2, 7), (0, 13)),
-    ("g", 0, 0): ((4, 1), (4, 2), (1, 9), (5, 1)),
-    ("d", 0, 0): ((5, 0),),
-    ("h", 2, 0): ((3, 4), (1, 10), (4, 3), (3, 5), (2, 8)),
-    ("h", 3, 0): ((2, 9), (1, 11), (5, 2), (0, 14), (0, 15)),
-    ("g", 1, 0): ((5, 3), (3, 6), (1, 12)),
-    ("g", 1, 1): ((4, 4), (3, 7), (2, 10), (4, 5), (1, 13), (5, 5), (0, 16)),
-    ("d", 1, 0): ((2, 11),),
-    ("h", 4, 0): ((4, 6), (2, 12), (1, 14), (0, 17)),
-    ("h", 5, 0): ((5, 4), (4, 7), (3, 8), (3, 9), (1, 15), (2, 13)),
-    ("g", 2, 0): ((5, 6), (2, 14), (1, 16)),
-    ("g", 2, 1): ((3, 10), (1, 17), (5, 7), (2, 15)),
-    ("e", 0, 0): ((3, 11), (0, 18), (3, 12), (2, 17), (2, 16), (4, 8), (4, 9), (0, 19), ("i", 0), ("s", 0), (4, 10), (1, 18), (1, 19), (3, 13), (4, 11), (3, 14), (5, 11), (2, 18), (5, 8), ("s", 1), (5, 9), (3, 15), (4, 12), (2, 19), ("s", 2), ("i", 1), (4, 15), (3, 16), (3, 17), (4, 13), (5, 12), (5, 10), ("s", 3), (4, 14), (3, 18), (5, 13), (3, 19), ("i", 2), (4, 16), (4, 17), (5, 15), ("s", 4), (5, 16), (5, 17), (4, 18), (5, 14), (4, 19), (5, 18), (5, 19)),
+    ("o", 2, 1): ((1, 3),),
+    ("s", 2, 0): ((2, 2),),
+    ("r", 0, 0): ((2, 3), (1, 4)),
+    ("r", 0, 1): ((1, 5),),
+    ("h", 0, 0): ((0, 7), (0, 8), (0, 9), (0, 10), (0, 11)),
+    ("h", 1, 0): ((3, 0), (3, 1), (2, 4), (2, 5), (1, 6)),
+    ("h", 2, 0): ((1, 7),),
+    ("h", 3, 0): ((3, 2),),
+    ("h", 4, 0): ((4, 0), (3, 3), (2, 6)),
+    ("h", 5, 0): ((4, 1), (2, 7), (1, 8)),
+    ("d", 0, 0): ((4, 2), (1, 9)),
+    ("i", 0, 0): ((5, 0), (5, 1), (4, 3), (3, 4), (2, 8), (1, 10), ("i", 0)),
+    ("a", 0, 0): ((5, 2), (3, 5), (2, 9), (1, 11), ("s", 0)),
+    ("g", 0, 0): ((5, 3), (3, 6), (2, 10)),
+    ("g", 1, 0): ((4, 4), (3, 7), (0, 12), ("s", 1)),
+    ("g", 2, 0): ((2, 11), (0, 13)),
+    ("e", 0, 0): (("s", 2), (4, 5), (3, 8), (5, 4), (1, 12), (0, 14), (4, 6), (5, 5), (4, 7), ("i", 1), (3, 9), (1, 13), (0, 15), (5, 6), (4, 8), (2, 12), (3, 10), (3, 11), (5, 7), ("s", 3), (1, 14), (2, 13), (0, 16), (1, 15), (5, 8), (1, 16), (2, 14), (2, 15), (4, 9), (2, 16), (4, 10), (5, 9), (3, 12), (4, 11), ("s", 4), (5, 10), ("i", 2), (3, 13), (5, 11), (4, 12), (3, 14), (3, 15), (4, 13), (3, 16), (4, 14), (5, 12), (4, 15), (4, 16), (5, 13), (5, 14), (5, 15), (5, 16)),
 }
 
 
@@ -774,8 +787,10 @@
     ]
     for copy in loads:
         copy.start()
-    for copy in loads[:2]:
+    for copy in loads:
         copy.wait()
+    for copy in moves:
+        copy.start()
     gq, gk, gv, go, gi, gf, gain_a, gain_f, table = held
     blocks = gq.shape[1] // LANES
     part_rows = blocks * LANES + GROUP * row_share
@@ -812,9 +827,6 @@
     table[...] = small[pl.ds(8, table.shape[0]), pl.ds(0, table.shape[1])]
     for index in (6, 7, 8):
         give(index)
-    for index in range(2):
-        loads[2 + index].wait()
-        moves[index].start()
     for copy in moves:
         copy.wait()
 
@@ -895,7 +907,6 @@
             vm(heads, block, vec_len),
             vm(16, vec_len, dtype=F32),
             vm(8, width, dtype=F32),
-            vm(3, length, WIDE),
             vm(length, 2 * length),
             vm(block, vec_len, dtype=F32),
             vm(SLOTS, 2, 2, 2, max(chunk_rows(row_share)), LANES),

time: 155 us -> 152 us (0.981)
  Pallas kernels: 154 us -> 151 us
    pallas_call x1, Pallas kernels: 150 us -> 146 us  [on_device(): pl.pallas_call(partial(layer_kernel, lo_count), out_shape=(jax.ShapeDtype...]
where the time goes in v1:
time: 152 us
  Pallas kernels  151 us (99%)
    pallas_call x1, Pallas kernels, on_device(): pl.pallas_call(partial(layer_kernel, lo_count), out_shape=(jax.ShapeDtype...  146 us
    pallas_call x1, Pallas kernels, on_device(): pl.pallas_call(partial(unpack_kernel, parts, row_share), out_shape=[jax.S...  4.34 us

profile of v1, /device:TPU:0, one launch (start us, length us, event | category | flops | bytes accessed | tf_op | source)
XLA Modules:
  0.0 151.6 jit_solution(659329796288989343)
XLA Ops:
  0.6 146.4 %shard_map.212 = (bf16[4,128,768]{2,1,0:T(8,128)(2,1)}, bf16[4,128,768]{2,1,0:T(8,128)(2,1)}, bf16[6912,128]{1,0:T(8,128)(2,1)}, f32[20,256]{1,0:T(8,128)}) custom-call(bf16[4,128,768]{2,1,0:T(8,128)(2,1)} %hidden.1, bf16[4,128,768]{2,1,0:T(8,128)(2,1)} %cot.1, s32[4]{0:T(128)} %query_len.1, s32[4]{0:T(128)} %doc_len.1, bf16[768,768]{1,0:T(8,128)(2,1)} %wq_hbm.1, ...), custom_call_target="tpu_custom_call" | custom-call | tf_op jit(solution)/shard_map/pallas_call | solution.py:872
  147.1 4.3 %shard_map.213 = (bf16[4,128,768]{2,1,0:T(8,128)(2,1)}, bf16[4,128,768]{2,1,0:T(8,128)(2,1)}, f32[96,768]{1,0:T(8,128)}, f32[96,768]{1,0:T(8,128)}, f32[96,768]{...) custom-call(bf16[6912,128]{1,0:T(8,128)(2,1)} %get-tuple-element.26., ...), custom_call_target="tpu_custom_call" | custom-call | tf_op jit(solution)/shard_map/pallas_call | solution.py:946

commit v2 on v1

--- a/solution.py
+++ b/solution.py
@@ -779,22 +779,25 @@
 def unpack_kernel(parts, row_share, shares_hbm, small_hbm, layer_in, grad_in_in, *refs):
     outs, held, (shares, small, through, sems, in_sems) = refs[:11], refs[11:20], refs[20:]
     moves = [pltpu.make_async_copy(through.at[index], outs[index], sems.at[index]) for index in range(2)]
-    loads = [
-        pltpu.make_async_copy(src, dst, in_sems.at[index])
-        for index, (src, dst) in enumerate(
-            ((shares_hbm, shares), (small_hbm, small), (layer_in, through.at[0]), (grad_in_in, through.at[1]))
-        )
-    ]
-    for copy in loads:
-        copy.start()
-    for copy in loads:
-        copy.wait()
-    for copy in moves:
-        copy.start()
     gq, gk, gv, go, gi, gf, gain_a, gain_f, table = held
     blocks = gq.shape[1] // LANES
     part_rows = blocks * LANES + GROUP * row_share
 
+    def load_share(index, rows):
+        place = pl.ds(index * part_rows, rows)
+        return pltpu.make_async_copy(shares_hbm.at[place], shares.at[place], in_sems.at[3 + index])
+
+    pieces = [load_share(part, part_rows) for part in range(parts)]
+    pieces.append(load_share(parts, shares.shape[0] - parts * part_rows))
+    others = [
+        pltpu.make_async_copy(src, dst, in_sems.at[index])
+        for index, (src, dst) in enumerate(
+            ((small_hbm, small), (layer_in, through.at[0]), (grad_in_in, through.at[1]))
+        )
+    ]
+    for copy in pieces + others:
+        copy.start()
+
     def take(start, rows):
         return shares[pl.ds(start, rows), :].astype(F32)
 
@@ -803,14 +806,21 @@
         moves[-1].start()
 
     for part in range(parts):
+        pieces[part].wait()
+        own_rows = pl.ds(part * LANES, LANES)
         for col in range(blocks):
-            gf[pl.ds(part * LANES, LANES), pl.ds(col * LANES, LANES)] = take(part * part_rows + col * LANES, LANES)
-    give(5)
-    for part in range(parts):
+            gf[own_rows, pl.ds(col * LANES, LANES)] = take(part * part_rows + col * LANES, LANES)
+        moves.append(pltpu.make_async_copy(gf.at[own_rows], outs[7].at[own_rows], sems.at[11 + part]))
+        moves[-1].start()
         base = part * part_rows + blocks * LANES
         for share in range(GROUP):
             gi[:, pl.ds((share * parts + part) * LANES, LANES)] = take(base + share * row_share, row_share)
     give(4)
+    for copy in others:
+        copy.wait()
+    for copy in moves[:2]:
+        copy.start()
+    pieces[parts].wait()
     base = parts * part_rows
     for col in range(blocks):
         go[:, pl.ds(col * LANES, LANES)] = take(base + col * row_share, row_share)
@@ -950,7 +960,7 @@
         in_specs=[hbm] * 4,
         out_specs=[hbm] * 11,
         scratch_shapes=[vm(*shape, dtype=F32) for shape in grad_shapes]
-        + [vm(total_rows, LANES), vm(small_rows, small_cols, dtype=F32), vm(2, *hidden_in.shape), dma(11), dma(4)],
+        + [vm(total_rows, LANES), vm(small_rows, small_cols, dtype=F32), vm(2, *hidden_in.shape), dma(11 + parts), dma(4 + parts)],
         compiler_params=pltpu.CompilerParams(vmem_limit_bytes=64 * 2**20 - 2**19),
     )(shares, small, layer_raw, grad_raw)
     if lo_count > 1:

time: 152 us -> 151 us (level)
  no operation moved by 1% of the time
where the time goes in v2:
time: 151 us
  Pallas kernels  150 us (99%)
    pallas_call x1, Pallas kernels, on_device(): pl.pallas_call(partial(layer_kernel, lo_count), out_shape=(jax.ShapeDtype...  146 us
    pallas_call x1, Pallas kernels, on_device(): pl.pallas_call(partial(unpack_kernel, parts, row_share), out_shape=[jax.S...  3.62 us

profile of v2, /device:TPU:0, one launch (start us, length us, event | category | flops | bytes accessed | tf_op | source)
XLA Modules:
  0.0 150.9 jit_solution(3814468005877428955)
XLA Ops:
  0.6 146.4 %shard_map.212 = (bf16[4,128,768]{2,1,0:T(8,128)(2,1)}, bf16[4,128,768]{2,1,0:T(8,128)(2,1)}, bf16[6912,128]{1,0:T(8,128)(2,1)}, f32[20,256]{1,0:T(8,128)}) custom-call(bf16[4,128,768]{2,1,0:T(8,128)(2,1)} %hidden.1, bf16[4,128,768]{2,1,0:T(8,128)(2,1)} %cot.1, s32[4]{0:T(128)} %query_len.1, s32[4]{0:T(128)} %doc_len.1, bf16[768,768]{1,0:T(8,128)(2,1)} %wq_hbm.1, ...), custom_call_target="tpu_custom_call" | custom-call | tf_op jit(solution)/shard_map/pallas_call | solution.py:882
  147.1 3.6 %shard_map.213 = (bf16[4,128,768]{2,1,0:T(8,128)(2,1)}, bf16[4,128,768]{2,1,0:T(8,128)(2,1)}, f32[96,768]{1,0:T(8,128)}, f32[96,768]{1,0:T(8,128)}, f32[96,768]{...) custom-call(bf16[6912,128]{1,0:T(8,128)(2,1)} %get-tuple-element.26., ...), custom_call_target="tpu_custom_call" | custom-call | tf_op jit(solution)/shard_map/pallas_call | solution.py:956

commit v3 on v2

--- a/solution.py
+++ b/solution.py
@@ -451,19 +451,21 @@
     gain_one = gain1[...].astype(F32).reshape(1, width)
     gain_two = gain2[...].astype(F32).reshape(1, width)
 
-    own_x.wait()
-    for other in row_devs:
-        x_arrived(other)
-    for index in range(len(row_devs)):
-        c_start(index)
-
     def norm_first(index):
         rows = at(index, block)
         values = x_row[rows, :].astype(F32)
         factor = lax.rsqrt(jnp.mean(values * values, axis=-1, keepdims=True) + EPS)
         n1[rows, :] = (values * factor * gain_one).astype(BF)
 
-    loop(seq_count, norm_first)
+    own_x.wait()
+    norm_first(sq)
+    for other in row_devs[:-1]:
+        x_arrived(other)
+        norm_first(other)
+    x_arrived(row_devs[-1])
+    for index in range(len(row_devs)):
+        c_start(index)
+    norm_first(row_devs[-1])
     for copy in square:
         copy.wait()
 

time: 151 us -> 151 us (level)
  no operation moved by 1% of the time
where the time goes in v3:
time: 151 us
  Pallas kernels  150 us (99%)
    pallas_call x1, Pallas kernels, on_device(): pl.pallas_call(partial(layer_kernel, lo_count), out_shape=(jax.ShapeDtype...  146 us
    pallas_call x1, Pallas kernels, on_device(): pl.pallas_call(partial(unpack_kernel, parts, row_share), out_shape=[jax.S...  3.62 us

profile of v3, /device:TPU:0, one launch (start us, length us, event | category | flops | bytes accessed | tf_op | source)
XLA Modules:
  0.0 150.7 jit_solution(2985725070261990359)
XLA Ops:
  0.6 146.3 %shard_map.212 = (bf16[4,128,768]{2,1,0:T(8,128)(2,1)}, bf16[4,128,768]{2,1,0:T(8,128)(2,1)}, bf16[6912,128]{1,0:T(8,128)(2,1)}, f32[20,256]{1,0:T(8,128)}) custom-call(bf16[4,128,768]{2,1,0:T(8,128)(2,1)} %hidden.1, bf16[4,128,768]{2,1,0:T(8,128)(2,1)} %cot.1, s32[4]{0:T(128)} %query_len.1, s32[4]{0:T(128)} %doc_len.1, bf16[768,768]{1,0:T(8,128)(2,1)} %wq_hbm.1, ...), custom_call_target="tpu_custom_call" | custom-call | tf_op jit(solution)/shard_map/pallas_call | solution.py:884
  146.9 3.6 %shard_map.213 = (bf16[4,128,768]{2,1,0:T(8,128)(2,1)}, bf16[4,128,768]{2,1,0:T(8,128)(2,1)}, f32[96,768]{1,0:T(8,128)}, f32[96,768]{1,0:T(8,128)}, f32[96,768]{...) custom-call(bf16[6912,128]{1,0:T(8,128)(2,1)} %get-tuple-element.26., ...), custom_call_target="tpu_custom_call" | custom-call | tf_op jit(solution)/shard_map/pallas_call | solution.py:958
